TPU v7x, 512 devices: a whole 4x8x8 slice. The times are simulated.
512 devices in a mesh: gx: 32 (over z, y_hi), gy: 16 (over y_lo, x, core).
Axes of the slice: x: 4, y: 8 (y_hi: 4, y_lo: 2; y = y_hi * 2 + y_lo), z: 8, core: 2. Of those that a mesh axis runs over, the one named last changes fastest.
Arguments:
- random_vectors: float32 [2, 256, 1024, 128], P(None, 'gx', 'gy'), may hold values from -6 to 6
- disorder: float32 [256, 1024, 128], P('gx', 'gy'), may hold values from -2 to 4
Outputs:
- moments: float32 [2, 10], replicated
- last_vectors: float32 [2, 256, 1024, 128], P(None, 'gx', 'gy')
All inputs are finite; a program needn't handle non-finite values.
Results may differ from a plain program's by a relative error of at most 0.0001.
Values sent between devices are 32-bit elements; how exact they have to be, the bound alone decides.
A program may use at most 64 MiB of HBM per device.

v0:
```python
import jax
import jax.numpy as jnp
from jax import lax
from jax.sharding import PartitionSpec as P

ITERS = 9


energy_scale = 10.5


def extended(shard, sides, width):
    for axis, dim in sides:
        devices, length = (lax.axis_size(axis), shard.shape[dim])
        up = [(i, (i + 1) % devices) for i in range(devices)]
        down = [(j, i) for i, j in up]
        last = lax.slice_in_dim(shard, length - width, length, axis=dim)
        initial = lax.slice_in_dim(shard, 0, width, axis=dim)
        before = lax.ppermute(last, axis, up)
        after = lax.ppermute(initial, axis, down)
        shard = jnp.concatenate([before, shard, after], axis=dim)
    return shard


def region_step(padded, energies):
    center = padded[:, 1:-1, 1:-1]
    beside = padded[:, 2:, 1:-1] + padded[:, :-2, 1:-1]
    beside = beside + padded[:, 1:-1, 2:] + padded[:, 1:-1, :-2]
    beside = beside + jnp.roll(center, -1, 3) + jnp.roll(center, 1, 3)
    return (energies * center - beside) / energy_scale


def local(random_vectors, disorder):
    sites = (
        random_vectors.shape[1]
        * lax.axis_size("gx")
        * random_vectors.shape[2]
        * lax.axis_size("gy")
        * random_vectors.shape[3]
    )
    totals_list = []

    def record(field):
        partial_sum = jnp.sum(random_vectors * field, axis=(1, 2, 3))
        totals_list.append(lax.psum(partial_sum, ("gx", "gy")))

    def single(field):
        padded = extended(field, (("gx", 1), ("gy", 2)), 1)
        return region_step(padded, disorder)

    record(random_vectors)
    previous = random_vectors
    current = single(random_vectors)
    record(current)
    for step in range(ITERS - 1):
        following = 2.0 * single(current) - previous
        previous, current = (current, following)
        record(current)
    moments = jnp.stack(totals_list, 1)
    return (moments / jnp.float32(sites), current)


def solution(mesh):
    placed = (P(None, "gx", "gy", None), P("gx", "gy", None))
    return jax.shard_map(
        local,
        mesh=mesh,
        in_specs=placed,
        out_specs=(P(), P(None, "gx", "gy", None)),
        check_vma=False,
    )
```

profile of v0, /device:TPU:6, one launch (start us, length us, event | category | flops | bytes accessed | tf_op | source)
XLA Modules:
  0.0 311.3 jit_solution(9784016708371355991)
XLA Ops:
  1.5 14.6 %collective-permute-start = (f32[2,1,64,128]{3,2,1,0:T(8,128)S(1)}, f32[2,1,64,128]{3,2,1,0:T(8,128)S(1)}, u32[]{:S(2)}, u32[]{:S(2)}) collective-permute-start(f32[2,1,64,128]{3,2,1,0:T(8,128)S(1)} %get-tuple-element.93), channel_id=1, source_target_pairs={{16,0},{32,16},{48,32},{64,48},{80,64},{96,80},{112,96},{128,112},... | collective-permute-start | bytes 196616 | tf_op jit(solution)/shard_map/ppermute | solution.py:20
  16.2 2.1 collective-permute-start.1
  19.9 6.8 %collective-permute-done.1 = f32[2,1,64,128]{3,2,1,0:T(8,128)S(1)} collective-permute-done((f32[2,1,64,128]{3,2,1,0:T(8,128)S(1)}, f32[2,1,64,128]{3,2,1,0:T(8,128)S(1)}, u32[]{:S(2)}, u32[]{:S(2)}) %collective-permute-start.1) | collective-permute-done | bytes 65568 | tf_op jit(solution)/shard_map/ppermute | solution.py:19
  26.8 1.9 collective-permute-start.2
  28.7 2.4 collective-permute-start.3
  31.2 2.5 collective-permute-done.3
  34.2 1.9 collective-permute-start.5
  36.2 8.1 %collective-permute-start.4 = (f32[2,1,64,128]{3,2,1,0:T(8,128)S(1)}, f32[2,1,64,128]{3,2,1,0:T(8,128)S(1)}, u32[]{:S(2)}, u32[]{:S(2)}) collective-permute-start(f32[2,1,64,128]{3,2,1,0:T(8,128)S(1)} %get-tuple-element.92), channel_id=1, source_target_pairs={{16,0},{32,16},{48,32},{64,48},{80,64},{96,80},{112,96},{128,112},... | collective-permute-start | bytes 196616 | tf_op jit(solution)/shard_map/ppermute | solution.py:20
  44.6 2.3 collective-permute-done.4
  47.0 1.9 collective-permute-start.6
  48.9 2.4 collective-permute-start.7
  51.5 2.4 collective-permute-done.7
  54.5 1.9 collective-permute-start.9
  56.4 8.6 %collective-permute-start.8 = (f32[2,1,64,128]{3,2,1,0:T(8,128)S(1)}, f32[2,1,64,128]{3,2,1,0:T(8,128)S(1)}, u32[]{:S(2)}, u32[]{:S(2)}) collective-permute-start(f32[2,1,64,128]{3,2,1,0:T(8,128)S(1)} %get-tuple-element.86), channel_id=1, source_target_pairs={{16,0},{32,16},{48,32},{64,48},{80,64},{96,80},{112,96},{128,112},... | collective-permute-start | bytes 196616 | tf_op jit(solution)/shard_map/ppermute | solution.py:20
  65.6 2.3 collective-permute-done.8
  67.8 1.9 collective-permute-start.10
  69.8 2.4 collective-permute-start.11
  72.4 2.4 collective-permute-done.11
  75.3 1.9 collective-permute-start.13
  77.2 8.8 %collective-permute-start.12 = (f32[2,1,64,128]{3,2,1,0:T(8,128)S(1)}, f32[2,1,64,128]{3,2,1,0:T(8,128)S(1)}, u32[]{:S(2)}, u32[]{:S(2)}) collective-permute-start(f32[2,1,64,128]{3,2,1,0:T(8,128)S(1)} %get-tuple-element.80), channel_id=1, source_target_pairs={{16,0},{32,16},{48,32},{64,48},{80,64},{96,80},{112,96},{128,112},... | collective-permute-start | bytes 196616 | tf_op jit(solution)/shard_map/ppermute | solution.py:20
  87.9 1.9 collective-permute-start.14
  89.8 3.8 %collective-permute-start.15 = (f32[2,10,1,128]{3,2,1,0:T(1,128)S(1)}, f32[2,10,1,128]{3,2,1,0:T(1,128)S(1)}, u32[]{:S(2)}, u32[]{:S(2)}) collective-permute-start(f32[2,10,1,128]{3,2,1,0:T(1,128)S(1)} %get-tuple-element.38), channel_id=1, source_target_pairs={{0,1},{1,2},{2,3},{3,4},{4,5},{5,6},{6,7},{7,8},{8,9},{9,10},{10,1... | collective-permute-start | bytes 30728 | tf_op jit(solution)/shard_map/ppermute | solution.py:19
  95.3 1.9 collective-permute-start.17
  97.2 8.5 %collective-permute-start.16 = (f32[2,1,64,128]{3,2,1,0:T(8,128)S(1)}, f32[2,1,64,128]{3,2,1,0:T(8,128)S(1)}, u32[]{:S(2)}, u32[]{:S(2)}) collective-permute-start(f32[2,1,64,128]{3,2,1,0:T(8,128)S(1)} %get-tuple-element.74), channel_id=1, source_target_pairs={{16,0},{32,16},{48,32},{64,48},{80,64},{96,80},{112,96},{128,112},... | collective-permute-start | bytes 196616 | tf_op jit(solution)/shard_map/ppermute | solution.py:20
  107.6 1.9 collective-permute-start.18
  109.5 5.9 %collective-permute-start.19 = (f32[2,10,1,128]{3,2,1,0:T(1,128)S(1)}, f32[2,10,1,128]{3,2,1,0:T(1,128)S(1)}, u32[]{:S(2)}, u32[]{:S(2)}) collective-permute-start(f32[2,10,1,128]{3,2,1,0:T(1,128)S(1)} %get-tuple-element.36), channel_id=1, source_target_pairs={{0,1},{1,2},{2,3},{3,4},{4,5},{5,6},{6,7},{7,8},{8,9},{9,10},{10,1... | collective-permute-start | bytes 30728 | tf_op jit(solution)/shard_map/ppermute | solution.py:19
  116.8 1.9 collective-permute-start.21
  118.7 8.3 %collective-permute-start.20 = (f32[2,1,64,128]{3,2,1,0:T(8,128)S(1)}, f32[2,1,64,128]{3,2,1,0:T(8,128)S(1)}, u32[]{:S(2)}, u32[]{:S(2)}) collective-permute-start(f32[2,1,64,128]{3,2,1,0:T(8,128)S(1)} %get-tuple-element.68), channel_id=1, source_target_pairs={{16,0},{32,16},{48,32},{64,48},{80,64},{96,80},{112,96},{128,112},... | collective-permute-start | bytes 196616 | tf_op jit(solution)/shard_map/ppermute | solution.py:20
  127.3 1.7 collective-permute-done.20
  129.0 1.9 collective-permute-start.22
  131.0 6.5 %collective-permute-start.23 = (f32[2,10,1,128]{3,2,1,0:T(1,128)S(1)}, f32[2,10,1,128]{3,2,1,0:T(1,128)S(1)}, u32[]{:S(2)}, u32[]{:S(2)}) collective-permute-start(f32[2,10,1,128]{3,2,1,0:T(1,128)S(1)} %get-tuple-element.34), channel_id=1, source_target_pairs={{0,1},{1,2},{2,3},{3,4},{4,5},{5,6},{6,7},{7,8},{8,9},{9,10},{10,1... | collective-permute-start | bytes 30728 | tf_op jit(solution)/shard_map/ppermute | solution.py:19
  138.8 1.9 collective-permute-start.25
  140.7 8.3 %collective-permute-start.24 = (f32[2,1,64,128]{3,2,1,0:T(8,128)S(1)}, f32[2,1,64,128]{3,2,1,0:T(8,128)S(1)}, u32[]{:S(2)}, u32[]{:S(2)}) collective-permute-start(f32[2,1,64,128]{3,2,1,0:T(8,128)S(1)} %get-tuple-element.62), channel_id=1, source_target_pairs={{16,0},{32,16},{48,32},{64,48},{80,64},{96,80},{112,96},{128,112},... | collective-permute-start | bytes 196616 | tf_op jit(solution)/shard_map/ppermute | solution.py:20
  149.3 1.6 collective-permute-done.24
  150.9 1.9 collective-permute-start.26
  152.8 6.5 %collective-permute-start.27 = (f32[2,10,1,128]{3,2,1,0:T(1,128)S(1)}, f32[2,10,1,128]{3,2,1,0:T(1,128)S(1)}, u32[]{:S(2)}, u32[]{:S(2)}) collective-permute-start(f32[2,10,1,128]{3,2,1,0:T(1,128)S(1)} %get-tuple-element.32), channel_id=1, source_target_pairs={{0,1},{1,2},{2,3},{3,4},{4,5},{5,6},{6,7},{7,8},{8,9},{9,10},{10,1... | collective-permute-start | bytes 30728 | tf_op jit(solution)/shard_map/ppermute | solution.py:19
  160.7 1.9 collective-permute-start.29
  162.6 8.2 %collective-permute-start.28 = (f32[2,1,64,128]{3,2,1,0:T(8,128)S(1)}, f32[2,1,64,128]{3,2,1,0:T(8,128)S(1)}, u32[]{:S(2)}, u32[]{:S(2)}) collective-permute-start(f32[2,1,64,128]{3,2,1,0:T(8,128)S(1)} %get-tuple-element.56), channel_id=1, source_target_pairs={{16,0},{32,16},{48,32},{64,48},{80,64},{96,80},{112,96},{128,112},... | collective-permute-start | bytes 196616 | tf_op jit(solution)/shard_map/ppermute | solution.py:20
  171.2 1.9 collective-permute-done.28
  173.1 1.9 collective-permute-start.30
  175.1 6.2 %collective-permute-start.31 = (f32[2,10,1,128]{3,2,1,0:T(1,128)S(1)}, f32[2,10,1,128]{3,2,1,0:T(1,128)S(1)}, u32[]{:S(2)}, u32[]{:S(2)}) collective-permute-start(f32[2,10,1,128]{3,2,1,0:T(1,128)S(1)} %get-tuple-element.30), channel_id=1, source_target_pairs={{0,1},{1,2},{2,3},{3,4},{4,5},{5,6},{6,7},{7,8},{8,9},{9,10},{10,1... | collective-permute-start | bytes 30728 | tf_op jit(solution)/shard_map/ppermute | solution.py:19
  182.6 1.9 collective-permute-start.33
  184.5 8.3 %collective-permute-start.32 = (f32[2,1,64,128]{3,2,1,0:T(8,128)S(1)}, f32[2,1,64,128]{3,2,1,0:T(8,128)S(1)}, u32[]{:S(2)}, u32[]{:S(2)}) collective-permute-start(f32[2,1,64,128]{3,2,1,0:T(8,128)S(1)} %get-tuple-element.46), channel_id=1, source_target_pairs={{16,0},{32,16},{48,32},{64,48},{80,64},{96,80},{112,96},{128,112},... | collective-permute-start | bytes 196616 | tf_op jit(solution)/shard_map/ppermute | solution.py:20
  193.1 2.1 collective-permute-done.32
  195.2 1.9 collective-permute-start.34
  197.2 6.5 %collective-permute-start.35 = (f32[2,10,1,128]{3,2,1,0:T(1,128)S(1)}, f32[2,10,1,128]{3,2,1,0:T(1,128)S(1)}, u32[]{:S(2)}, u32[]{:S(2)}) collective-permute-start(f32[2,10,1,128]{3,2,1,0:T(1,128)S(1)} %get-tuple-element.28), channel_id=1, source_target_pairs={{0,1},{1,2},{2,3},{3,4},{4,5},{5,6},{6,7},{7,8},{8,9},{9,10},{10,1... | collective-permute-start | bytes 30728 | tf_op jit(solution)/shard_map/ppermute | solution.py:19
  204.5 1.7 multiply_reduce_fusion
  206.1 103.6 %all-reduce = (f32[2,1]{0,1:T(1,128)S(1)}, f32[2,1]{0,1:T(1,128)S(1)}, f32[2,1]{0,1:T(1,128)S(1)}, f32[2,1]{0,1:T(1,128)S(1)}, f32[2,1]{0,1:T(1,128)S(1)}, /*ind...) all-reduce(f32[2,1]{0,1:T(1,128)S(1)} %bitcast.18, ...), channel_id=1, replica_groups=mesh['gx'=32,'gy'=16] {'gx','gy'}, use_global_device_ids=true, to_apply=%region_1.0 | all-reduce | flops 20 | bytes 160 | tf_op jit(solution)/shard_map/psum | solution.py:45
  (90 shorter events, 20.0 us)
Async XLA Ops:
  1.5 25.2 %collective-permute-start = (f32[2,1,64,128]{3,2,1,0:T(8,128)S(1)}, f32[2,1,64,128]{3,2,1,0:T(8,128)S(1)}, u32[]{:S(2)}, u32[]{:S(2)}) collective-permute-start(f32[2,1,64,128]{3,2,1,0:T(8,128)S(1)} %get-tuple-element.93), channel_id=1, source_target_pairs={{16,0},{32,16},{48,32},{64,48},{80,64},{96,80},{112,96},{128,112},... | collective-permute-start | bytes 196616 | tf_op jit(solution)/shard_map/ppermute | solution.py:20
  16.2 3.5 %copy-start = (f32[2,8,64,128]{3,2,1,0:T(8,128)S(1)}, f32[2,8,64,128]{3,2,1,0:T(8,128)}, u32[]{:S(2)}) copy-start(f32[2,8,64,128]{3,2,1,0:T(8,128)} %param.2) | copy-start | bytes 1572868
  16.2 10.5 %collective-permute-start.1 = (f32[2,1,64,128]{3,2,1,0:T(8,128)S(1)}, f32[2,1,64,128]{3,2,1,0:T(8,128)S(1)}, u32[]{:S(2)}, u32[]{:S(2)}) collective-permute-start(f32[2,1,64,128]{3,2,1,0:T(8,128)S(1)} %get-tuple-element.94), channel_id=1, source_target_pairs={{0,16},{16,32},{32,48},{48,64},{64,80},{80,96},{96,112},{112,128},... | collective-permute-start | bytes 196616 | tf_op jit(solution)/shard_map/ppermute | solution.py:19
  26.7 4.4 %copy-start.1 = (f32[8,64,128]{2,1,0:T(8,128)S(1)}, f32[8,64,128]{2,1,0:T(8,128)}, u32[]{:S(2)}) copy-start(f32[8,64,128]{2,1,0:T(8,128)} %param.3) | copy-start | bytes 786436
  26.8 4.4 %collective-permute-start.2 = (f32[2,10,1,128]{3,2,1,0:T(1,128)S(1)}, f32[2,10,1,128]{3,2,1,0:T(1,128)S(1)}, u32[]{:S(2)}, u32[]{:S(2)}) collective-permute-start(f32[2,10,1,128]{3,2,1,0:T(1,128)S(1)} %get-tuple-element.43), channel_id=1, source_target_pairs={{1,0},{2,1},{3,2},{4,3},{5,4},{6,5},{7,6},{8,7},{9,8},{10,9},{11,1... | collective-permute-start | bytes 30728 | tf_op jit(solution)/shard_map/ppermute | solution.py:20
  28.7 5.0 %collective-permute-start.3 = (f32[2,10,1,128]{3,2,1,0:T(1,128)S(1)}, f32[2,10,1,128]{3,2,1,0:T(1,128)S(1)}, u32[]{:S(2)}, u32[]{:S(2)}) collective-permute-start(f32[2,10,1,128]{3,2,1,0:T(1,128)S(1)} %get-tuple-element.44), channel_id=1, source_target_pairs={{0,1},{1,2},{2,3},{3,4},{4,5},{5,6},{6,7},{7,8},{8,9},{9,10},{10,1... | collective-permute-start | bytes 30728 | tf_op jit(solution)/shard_map/ppermute | solution.py:19
  34.2 10.4 %collective-permute-start.5 = (f32[2,1,64,128]{3,2,1,0:T(8,128)S(1)}, f32[2,1,64,128]{3,2,1,0:T(8,128)S(1)}, u32[]{:S(2)}, u32[]{:S(2)}) collective-permute-start(f32[2,1,64,128]{3,2,1,0:T(8,128)S(1)} %get-tuple-element.91), channel_id=1, source_target_pairs={{0,16},{16,32},{32,48},{48,64},{64,80},{80,96},{96,112},{112,128},... | collective-permute-start | bytes 196616 | tf_op jit(solution)/shard_map/ppermute | solution.py:19
  36.2 10.8 %collective-permute-start.4 = (f32[2,1,64,128]{3,2,1,0:T(8,128)S(1)}, f32[2,1,64,128]{3,2,1,0:T(8,128)S(1)}, u32[]{:S(2)}, u32[]{:S(2)}) collective-permute-start(f32[2,1,64,128]{3,2,1,0:T(8,128)S(1)} %get-tuple-element.92), channel_id=1, source_target_pairs={{16,0},{32,16},{48,32},{64,48},{80,64},{96,80},{112,96},{128,112},... | collective-permute-start | bytes 196616 | tf_op jit(solution)/shard_map/ppermute | solution.py:20
  47.0 4.6 %collective-permute-start.6 = (f32[2,10,1,128]{3,2,1,0:T(1,128)S(1)}, f32[2,10,1,128]{3,2,1,0:T(1,128)S(1)}, u32[]{:S(2)}, u32[]{:S(2)}) collective-permute-start(f32[2,10,1,128]{3,2,1,0:T(1,128)S(1)} %get-tuple-element.41), channel_id=1, source_target_pairs={{1,0},{2,1},{3,2},{4,3},{5,4},{6,5},{7,6},{8,7},{9,8},{10,9},{11,1... | collective-permute-start | bytes 30728 | tf_op jit(solution)/shard_map/ppermute | solution.py:20
  48.9 5.0 %collective-permute-start.7 = (f32[2,10,1,128]{3,2,1,0:T(1,128)S(1)}, f32[2,10,1,128]{3,2,1,0:T(1,128)S(1)}, u32[]{:S(2)}, u32[]{:S(2)}) collective-permute-start(f32[2,10,1,128]{3,2,1,0:T(1,128)S(1)} %get-tuple-element.42), channel_id=1, source_target_pairs={{0,1},{1,2},{2,3},{3,4},{4,5},{5,6},{6,7},{7,8},{8,9},{9,10},{10,1... | collective-permute-start | bytes 30728 | tf_op jit(solution)/shard_map/ppermute | solution.py:19
  54.5 11.1 %collective-permute-start.9 = (f32[2,1,64,128]{3,2,1,0:T(8,128)S(1)}, f32[2,1,64,128]{3,2,1,0:T(8,128)S(1)}, u32[]{:S(2)}, u32[]{:S(2)}) collective-permute-start(f32[2,1,64,128]{3,2,1,0:T(8,128)S(1)} %get-tuple-element.85), channel_id=1, source_target_pairs={{0,16},{16,32},{32,48},{48,64},{64,80},{80,96},{96,112},{112,128},... | collective-permute-start | bytes 196616 | tf_op jit(solution)/shard_map/ppermute | solution.py:19
  56.4 11.4 %collective-permute-start.8 = (f32[2,1,64,128]{3,2,1,0:T(8,128)S(1)}, f32[2,1,64,128]{3,2,1,0:T(8,128)S(1)}, u32[]{:S(2)}, u32[]{:S(2)}) collective-permute-start(f32[2,1,64,128]{3,2,1,0:T(8,128)S(1)} %get-tuple-element.86), channel_id=1, source_target_pairs={{16,0},{32,16},{48,32},{64,48},{80,64},{96,80},{112,96},{128,112},... | collective-permute-start | bytes 196616 | tf_op jit(solution)/shard_map/ppermute | solution.py:20
  67.8 4.6 %collective-permute-start.10 = (f32[2,10,1,128]{3,2,1,0:T(1,128)S(1)}, f32[2,10,1,128]{3,2,1,0:T(1,128)S(1)}, u32[]{:S(2)}, u32[]{:S(2)}) collective-permute-start(f32[2,10,1,128]{3,2,1,0:T(1,128)S(1)} %get-tuple-element.39), channel_id=1, source_target_pairs={{1,0},{2,1},{3,2},{4,3},{5,4},{6,5},{7,6},{8,7},{9,8},{10,9},{11,1... | collective-permute-start | bytes 30728 | tf_op jit(solution)/shard_map/ppermute | solution.py:20
  69.8 5.0 %collective-permute-start.11 = (f32[2,10,1,128]{3,2,1,0:T(1,128)S(1)}, f32[2,10,1,128]{3,2,1,0:T(1,128)S(1)}, u32[]{:S(2)}, u32[]{:S(2)}) collective-permute-start(f32[2,10,1,128]{3,2,1,0:T(1,128)S(1)} %get-tuple-element.40), channel_id=1, source_target_pairs={{0,1},{1,2},{2,3},{3,4},{4,5},{5,6},{6,7},{7,8},{8,9},{9,10},{10,1... | collective-permute-start | bytes 30728 | tf_op jit(solution)/shard_map/ppermute | solution.py:19
  75.3 11.3 %collective-permute-start.13 = (f32[2,1,64,128]{3,2,1,0:T(8,128)S(1)}, f32[2,1,64,128]{3,2,1,0:T(8,128)S(1)}, u32[]{:S(2)}, u32[]{:S(2)}) collective-permute-start(f32[2,1,64,128]{3,2,1,0:T(8,128)S(1)} %get-tuple-element.79), channel_id=1, source_target_pairs={{0,16},{16,32},{32,48},{48,64},{64,80},{80,96},{96,112},{112,128},... | collective-permute-start | bytes 196616 | tf_op jit(solution)/shard_map/ppermute | solution.py:19
  77.2 10.6 %collective-permute-start.12 = (f32[2,1,64,128]{3,2,1,0:T(8,128)S(1)}, f32[2,1,64,128]{3,2,1,0:T(8,128)S(1)}, u32[]{:S(2)}, u32[]{:S(2)}) collective-permute-start(f32[2,1,64,128]{3,2,1,0:T(8,128)S(1)} %get-tuple-element.80), channel_id=1, source_target_pairs={{16,0},{32,16},{48,32},{64,48},{80,64},{96,80},{112,96},{128,112},... | collective-permute-start | bytes 196616 | tf_op jit(solution)/shard_map/ppermute | solution.py:20
  87.9 5.9 %collective-permute-start.14 = (f32[2,10,1,128]{3,2,1,0:T(1,128)S(1)}, f32[2,10,1,128]{3,2,1,0:T(1,128)S(1)}, u32[]{:S(2)}, u32[]{:S(2)}) collective-permute-start(f32[2,10,1,128]{3,2,1,0:T(1,128)S(1)} %get-tuple-element.37), channel_id=1, source_target_pairs={{1,0},{2,1},{3,2},{4,3},{5,4},{6,5},{7,6},{8,7},{9,8},{10,9},{11,1... | collective-permute-start | bytes 30728 | tf_op jit(solution)/shard_map/ppermute | solution.py:20
  89.8 5.0 %collective-permute-start.15 = (f32[2,10,1,128]{3,2,1,0:T(1,128)S(1)}, f32[2,10,1,128]{3,2,1,0:T(1,128)S(1)}, u32[]{:S(2)}, u32[]{:S(2)}) collective-permute-start(f32[2,10,1,128]{3,2,1,0:T(1,128)S(1)} %get-tuple-element.38), channel_id=1, source_target_pairs={{0,1},{1,2},{2,3},{3,4},{4,5},{5,6},{6,7},{7,8},{8,9},{9,10},{10,1... | collective-permute-start | bytes 30728 | tf_op jit(solution)/shard_map/ppermute | solution.py:19
  95.3 11.5 %collective-permute-start.17 = (f32[2,1,64,128]{3,2,1,0:T(8,128)S(1)}, f32[2,1,64,128]{3,2,1,0:T(8,128)S(1)}, u32[]{:S(2)}, u32[]{:S(2)}) collective-permute-start(f32[2,1,64,128]{3,2,1,0:T(8,128)S(1)} %get-tuple-element.73), channel_id=1, source_target_pairs={{0,16},{16,32},{32,48},{48,64},{64,80},{80,96},{96,112},{112,128},... | collective-permute-start | bytes 196616 | tf_op jit(solution)/shard_map/ppermute | solution.py:19
  97.2 10.4 %collective-permute-start.16 = (f32[2,1,64,128]{3,2,1,0:T(8,128)S(1)}, f32[2,1,64,128]{3,2,1,0:T(8,128)S(1)}, u32[]{:S(2)}, u32[]{:S(2)}) collective-permute-start(f32[2,1,64,128]{3,2,1,0:T(8,128)S(1)} %get-tuple-element.74), channel_id=1, source_target_pairs={{16,0},{32,16},{48,32},{64,48},{80,64},{96,80},{112,96},{128,112},... | collective-permute-start | bytes 196616 | tf_op jit(solution)/shard_map/ppermute | solution.py:20
  107.6 8.0 %collective-permute-start.18 = (f32[2,10,1,128]{3,2,1,0:T(1,128)S(1)}, f32[2,10,1,128]{3,2,1,0:T(1,128)S(1)}, u32[]{:S(2)}, u32[]{:S(2)}) collective-permute-start(f32[2,10,1,128]{3,2,1,0:T(1,128)S(1)} %get-tuple-element.35), channel_id=1, source_target_pairs={{1,0},{2,1},{3,2},{4,3},{5,4},{6,5},{7,6},{8,7},{9,8},{10,9},{11,1... | collective-permute-start | bytes 30728 | tf_op jit(solution)/shard_map/ppermute | solution.py:20
  109.5 6.7 %collective-permute-start.19 = (f32[2,10,1,128]{3,2,1,0:T(1,128)S(1)}, f32[2,10,1,128]{3,2,1,0:T(1,128)S(1)}, u32[]{:S(2)}, u32[]{:S(2)}) collective-permute-start(f32[2,10,1,128]{3,2,1,0:T(1,128)S(1)} %get-tuple-element.36), channel_id=1, source_target_pairs={{0,1},{1,2},{2,3},{3,4},{4,5},{5,6},{6,7},{7,8},{8,9},{9,10},{10,1... | collective-permute-start | bytes 30728 | tf_op jit(solution)/shard_map/ppermute | solution.py:19
  116.8 10.6 %collective-permute-start.21 = (f32[2,1,64,128]{3,2,1,0:T(8,128)S(1)}, f32[2,1,64,128]{3,2,1,0:T(8,128)S(1)}, u32[]{:S(2)}, u32[]{:S(2)}) collective-permute-start(f32[2,1,64,128]{3,2,1,0:T(8,128)S(1)} %get-tuple-element.67), channel_id=1, source_target_pairs={{0,16},{16,32},{32,48},{48,64},{64,80},{80,96},{96,112},{112,128},... | collective-permute-start | bytes 196616 | tf_op jit(solution)/shard_map/ppermute | solution.py:19
  118.7 10.3 %collective-permute-start.20 = (f32[2,1,64,128]{3,2,1,0:T(8,128)S(1)}, f32[2,1,64,128]{3,2,1,0:T(8,128)S(1)}, u32[]{:S(2)}, u32[]{:S(2)}) collective-permute-start(f32[2,1,64,128]{3,2,1,0:T(8,128)S(1)} %get-tuple-element.68), channel_id=1, source_target_pairs={{16,0},{32,16},{48,32},{64,48},{80,64},{96,80},{112,96},{128,112},... | collective-permute-start | bytes 196616 | tf_op jit(solution)/shard_map/ppermute | solution.py:20
  129.0 8.6 %collective-permute-start.22 = (f32[2,10,1,128]{3,2,1,0:T(1,128)S(1)}, f32[2,10,1,128]{3,2,1,0:T(1,128)S(1)}, u32[]{:S(2)}, u32[]{:S(2)}) collective-permute-start(f32[2,10,1,128]{3,2,1,0:T(1,128)S(1)} %get-tuple-element.33), channel_id=1, source_target_pairs={{1,0},{2,1},{3,2},{4,3},{5,4},{6,5},{7,6},{8,7},{9,8},{10,9},{11,1... | collective-permute-start | bytes 30728 | tf_op jit(solution)/shard_map/ppermute | solution.py:20
  131.0 7.3 %collective-permute-start.23 = (f32[2,10,1,128]{3,2,1,0:T(1,128)S(1)}, f32[2,10,1,128]{3,2,1,0:T(1,128)S(1)}, u32[]{:S(2)}, u32[]{:S(2)}) collective-permute-start(f32[2,10,1,128]{3,2,1,0:T(1,128)S(1)} %get-tuple-element.34), channel_id=1, source_target_pairs={{0,1},{1,2},{2,3},{3,4},{4,5},{5,6},{6,7},{7,8},{8,9},{9,10},{10,1... | collective-permute-start | bytes 30728 | tf_op jit(solution)/shard_map/ppermute | solution.py:19
  138.8 10.5 %collective-permute-start.25 = (f32[2,1,64,128]{3,2,1,0:T(8,128)S(1)}, f32[2,1,64,128]{3,2,1,0:T(8,128)S(1)}, u32[]{:S(2)}, u32[]{:S(2)}) collective-permute-start(f32[2,1,64,128]{3,2,1,0:T(8,128)S(1)} %get-tuple-element.61), channel_id=1, source_target_pairs={{0,16},{16,32},{32,48},{48,64},{64,80},{80,96},{96,112},{112,128},... | collective-permute-start | bytes 196616 | tf_op jit(solution)/shard_map/ppermute | solution.py:19
  140.7 10.2 %collective-permute-start.24 = (f32[2,1,64,128]{3,2,1,0:T(8,128)S(1)}, f32[2,1,64,128]{3,2,1,0:T(8,128)S(1)}, u32[]{:S(2)}, u32[]{:S(2)}) collective-permute-start(f32[2,1,64,128]{3,2,1,0:T(8,128)S(1)} %get-tuple-element.62), channel_id=1, source_target_pairs={{16,0},{32,16},{48,32},{64,48},{80,64},{96,80},{112,96},{128,112},... | collective-permute-start | bytes 196616 | tf_op jit(solution)/shard_map/ppermute | solution.py:20
  150.9 8.7 %collective-permute-start.26 = (f32[2,10,1,128]{3,2,1,0:T(1,128)S(1)}, f32[2,10,1,128]{3,2,1,0:T(1,128)S(1)}, u32[]{:S(2)}, u32[]{:S(2)}) collective-permute-start(f32[2,10,1,128]{3,2,1,0:T(1,128)S(1)} %get-tuple-element.31), channel_id=1, source_target_pairs={{1,0},{2,1},{3,2},{4,3},{5,4},{6,5},{7,6},{8,7},{9,8},{10,9},{11,1... | collective-permute-start | bytes 30728 | tf_op jit(solution)/shard_map/ppermute | solution.py:20
  152.8 7.3 %collective-permute-start.27 = (f32[2,10,1,128]{3,2,1,0:T(1,128)S(1)}, f32[2,10,1,128]{3,2,1,0:T(1,128)S(1)}, u32[]{:S(2)}, u32[]{:S(2)}) collective-permute-start(f32[2,10,1,128]{3,2,1,0:T(1,128)S(1)} %get-tuple-element.32), channel_id=1, source_target_pairs={{0,1},{1,2},{2,3},{3,4},{4,5},{5,6},{6,7},{7,8},{8,9},{9,10},{10,1... | collective-permute-start | bytes 30728 | tf_op jit(solution)/shard_map/ppermute | solution.py:19
  160.7 10.5 %collective-permute-start.29 = (f32[2,1,64,128]{3,2,1,0:T(8,128)S(1)}, f32[2,1,64,128]{3,2,1,0:T(8,128)S(1)}, u32[]{:S(2)}, u32[]{:S(2)}) collective-permute-start(f32[2,1,64,128]{3,2,1,0:T(8,128)S(1)} %get-tuple-element.55), channel_id=1, source_target_pairs={{0,16},{16,32},{32,48},{48,64},{64,80},{80,96},{96,112},{112,128},... | collective-permute-start | bytes 196616 | tf_op jit(solution)/shard_map/ppermute | solution.py:19
  162.6 10.5 %collective-permute-start.28 = (f32[2,1,64,128]{3,2,1,0:T(8,128)S(1)}, f32[2,1,64,128]{3,2,1,0:T(8,128)S(1)}, u32[]{:S(2)}, u32[]{:S(2)}) collective-permute-start(f32[2,1,64,128]{3,2,1,0:T(8,128)S(1)} %get-tuple-element.56), channel_id=1, source_target_pairs={{16,0},{32,16},{48,32},{64,48},{80,64},{96,80},{112,96},{128,112},... | collective-permute-start | bytes 196616 | tf_op jit(solution)/shard_map/ppermute | solution.py:20
  173.1 8.3 %collective-permute-start.30 = (f32[2,10,1,128]{3,2,1,0:T(1,128)S(1)}, f32[2,10,1,128]{3,2,1,0:T(1,128)S(1)}, u32[]{:S(2)}, u32[]{:S(2)}) collective-permute-start(f32[2,10,1,128]{3,2,1,0:T(1,128)S(1)} %get-tuple-element.29), channel_id=1, source_target_pairs={{1,0},{2,1},{3,2},{4,3},{5,4},{6,5},{7,6},{8,7},{9,8},{10,9},{11,1... | collective-permute-start | bytes 30728 | tf_op jit(solution)/shard_map/ppermute | solution.py:20
  175.1 7.0 %collective-permute-start.31 = (f32[2,10,1,128]{3,2,1,0:T(1,128)S(1)}, f32[2,10,1,128]{3,2,1,0:T(1,128)S(1)}, u32[]{:S(2)}, u32[]{:S(2)}) collective-permute-start(f32[2,10,1,128]{3,2,1,0:T(1,128)S(1)} %get-tuple-element.30), channel_id=1, source_target_pairs={{0,1},{1,2},{2,3},{3,4},{4,5},{5,6},{6,7},{7,8},{8,9},{9,10},{10,1... | collective-permute-start | bytes 30728 | tf_op jit(solution)/shard_map/ppermute | solution.py:19
  182.6 10.5 %collective-permute-start.33 = (f32[2,1,64,128]{3,2,1,0:T(8,128)S(1)}, f32[2,1,64,128]{3,2,1,0:T(8,128)S(1)}, u32[]{:S(2)}, u32[]{:S(2)}) collective-permute-start(f32[2,1,64,128]{3,2,1,0:T(8,128)S(1)} %get-tuple-element.45), channel_id=1, source_target_pairs={{0,16},{16,32},{32,48},{48,64},{64,80},{80,96},{96,112},{112,128},... | collective-permute-start | bytes 196616 | tf_op jit(solution)/shard_map/ppermute | solution.py:19
  184.5 10.7 %collective-permute-start.32 = (f32[2,1,64,128]{3,2,1,0:T(8,128)S(1)}, f32[2,1,64,128]{3,2,1,0:T(8,128)S(1)}, u32[]{:S(2)}, u32[]{:S(2)}) collective-permute-start(f32[2,1,64,128]{3,2,1,0:T(8,128)S(1)} %get-tuple-element.46), channel_id=1, source_target_pairs={{16,0},{32,16},{48,32},{64,48},{80,64},{96,80},{112,96},{128,112},... | collective-permute-start | bytes 196616 | tf_op jit(solution)/shard_map/ppermute | solution.py:20
  195.2 8.6 %collective-permute-start.34 = (f32[2,10,1,128]{3,2,1,0:T(1,128)S(1)}, f32[2,10,1,128]{3,2,1,0:T(1,128)S(1)}, u32[]{:S(2)}, u32[]{:S(2)}) collective-permute-start(f32[2,10,1,128]{3,2,1,0:T(1,128)S(1)} %get-tuple-element.27), channel_id=1, source_target_pairs={{1,0},{2,1},{3,2},{4,3},{5,4},{6,5},{7,6},{8,7},{9,8},{10,9},{11,1... | collective-permute-start | bytes 30728 | tf_op jit(solution)/shard_map/ppermute | solution.py:20
  197.2 7.3 %collective-permute-start.35 = (f32[2,10,1,128]{3,2,1,0:T(1,128)S(1)}, f32[2,10,1,128]{3,2,1,0:T(1,128)S(1)}, u32[]{:S(2)}, u32[]{:S(2)}) collective-permute-start(f32[2,10,1,128]{3,2,1,0:T(1,128)S(1)} %get-tuple-element.28), channel_id=1, source_target_pairs={{0,1},{1,2},{2,3},{3,4},{4,5},{5,6},{6,7},{7,8},{8,9},{9,10},{10,1... | collective-permute-start | bytes 30728 | tf_op jit(solution)/shard_map/ppermute | solution.py:19
where the time goes:
time: 314 us; the launch traced here: 311 us
  starting transfers between devices  159 us (51%)
  blocking collectives  104 us (33%)
  waiting for transfers between devices  34.1 us (11%)
  local copies, waits for them, and re-layouts  7.07 us (2%)
  other arithmetic  6.41 us (2%)
    psum x1, blocking collectives, record(): totals_list.append(lax.psum(partial_sum, ('gx', 'gy')))  104 us
    ppermute x18, starting transfers between devices, extended(): after = lax.ppermute(initial, axis, down)  99 us
    ppermute x18, starting transfers between devices, extended(): before = lax.ppermute(last, axis, up)  60 us
    ppermute x18, waiting for transfers between devices, extended(): before = lax.ppermute(last, axis, up)  20.1 us
    ppermute x18, waiting for transfers between devices, extended(): after = lax.ppermute(initial, axis, down)  13.9 us
  transfers between devices with their start and end apart: 36, of which 26 were waited for; matrix products, arithmetic and copies ran while one was open for 2% of the time, Pallas kernels for 0%

commit v1 on v0

v1 whole, which is shorter than its diff:
```python
import functools

import jax
import jax.numpy as jnp
from jax import lax
from jax.experimental import pallas as pl
from jax.experimental.pallas import tpu as pltpu
from jax.sharding import PartitionSpec as P

MESH = pl.DeviceIdType.MESH
ITERS = 9
ENERGY_SCALE = 10.5
TILE = 8
HALO = 3
ROW0 = 2 * TILE
WIDTHS = (3, 2, 2, 2)
SIDES = ((-1, 0), (1, 0), (0, -1), (0, 1), (-1, -1), (-1, 1), (1, -1), (1, 1))
X_SIDES = (0, 1, 4, 5, 6, 7)
Y_SIDES = (2, 3)
GROUP = 8


def body(start_ref, disorder_ref, moments_ref, last_ref, v, energy, sums, partial, local_sem, send_sem, recv_sem, sum_send, sum_recv):
    _, nx, ny, nz = start_ref.shape
    sx, sy = lax.axis_size("gx"), lax.axis_size("gy")
    gx, gy = lax.axis_index("gx"), lax.axis_index("gy")
    x_first, x_end = HALO, HALO + nx
    y_end = ROW0 + ny
    sites = nx * ny * nz * sx * sy

    def beside(dx, dy):
        return (lax.rem(gx + sx + dx, sx), lax.rem(gy + sy + dy, sy))

    z, y_hi = gx // 4, gx % 4
    y_lo, xc = gy // GROUP, gy % GROUP
    y = y_hi * 2 + y_lo
    places = (xc, y, z)

    def partner(turn, d):
        if turn == 0:
            return (gx, y_lo * GROUP + (xc + d) % GROUP)
        if turn == 1:
            to = (y + d) % GROUP
            return (z * 4 + to // 2, (to % 2) * GROUP + xc)
        return (((z + d) % GROUP) * 4 + y_hi, gy)

    barrier = pltpu.get_barrier_semaphore()
    for dx, dy in SIDES:
        pl.semaphore_signal(barrier, inc=1, device_id=beside(dx, dy), device_id_type=MESH)
    for turn in range(3):
        for d in range(1, GROUP):
            pl.semaphore_signal(barrier, inc=1, device_id=partner(turn, d), device_id_type=MESH)

    own = [pltpu.make_async_copy(start_ref.at[k], v.at[k, 0, pl.ds(x_first, nx), pl.ds(ROW0, ny)], local_sem.at[k]) for k in range(2)]
    own.append(pltpu.make_async_copy(disorder_ref, energy.at[pl.ds(x_first, nx), pl.ds(ROW0, ny)], local_sem.at[2]))
    for copy in own:
        copy.start()
    pl.semaphore_wait(barrier, len(SIDES) + 3 * (GROUP - 1))

    buffers = (0, 2, 1, 2)

    def message(e, k, side):
        dx, dy = SIDES[side]
        width = WIDTHS[e] - (k == 2) - (dx != 0 and dy != 0)
        x_from, x_size, x_to = {
            -1: (0, width, x_end),
            0: (0, nx, x_first),
            1: (nx - width, width, x_first - width),
        }[dx]
        y_from, y_size, y_to = {
            -1: (0, TILE, y_end),
            0: (0, ny, ROW0),
            1: (ny - TILE, TILE, ROW0 - TILE),
        }[dy]
        here = (pl.ds(x_from, x_size), pl.ds(y_from, y_size))
        there = (pl.ds(x_to, x_size), pl.ds(y_to, y_size))
        if k == 2:
            src, dst = disorder_ref.at[here], energy.at[there]
        else:
            b = buffers[e]
            if e == 0:
                src = start_ref.at[(k, *here)]
            else:
                src = v.at[k, b, pl.ds(x_first + x_from, x_size), pl.ds(ROW0 + y_from, y_size)]
            dst = v.at[(k, b, *there)]
        return pltpu.make_async_remote_copy(
            src_ref=src,
            dst_ref=dst,
            send_sem=send_sem.at[e, k, side],
            recv_sem=recv_sem.at[e, k, side],
            device_id=beside(dx, dy),
            device_id_type=MESH,
        )

    def send(e, k):
        for side in range(len(SIDES)):
            message(e, k, side).start()

    def arrived(e, k, sides):
        for side in sides:
            message(e, k, side).wait_recv()

    def sent(e, k):
        for side in range(len(SIDES)):
            message(e, k, side).wait_send()

    def advance(k, now, before, after, x0, x1, wide, moment=None):
        r0, r1 = (ROW0 - TILE, y_end + TILE) if wide else (ROW0, y_end)
        factor = (1.0 if before is None else 2.0) / ENERGY_SCALE

        def layer(x, totals):
            for r in range(r0, r1, TILE):
                rows = pl.ds(r, TILE)
                center = v[k, now, x, rows, :]
                total = v[k, now, x + 1, rows, :] + v[k, now, x - 1, rows, :]
                total = total + v[k, now, x, pl.ds(r + 1, TILE), :] + v[k, now, x, pl.ds(r - 1, TILE), :]
                total = total + pltpu.roll(center, nz - 1, 1) + pltpu.roll(center, 1, 1)
                result = (energy[x, rows, :] * center - total) * factor
                if before is not None:
                    result = result - v[k, before, x, rows, :]
                v[k, after, x, rows, :] = result
                if moment is not None and ROW0 <= r < y_end:
                    totals = (totals[0] + center * center, totals[1] + center * result)
            return totals

        zero = jnp.zeros((TILE, nz), jnp.float32)
        totals = lax.fori_loop(x0, x1, layer, (zero, zero))
        if moment is not None:
            for i in range(2):
                sums[k, 2 * moment + i] += totals[i]

    sums[...] = jnp.zeros_like(sums)
    send(0, 0)
    send(0, 2)
    send(0, 1)

    for k in range(2):
        own[k].wait()
        arrived(0, k, range(len(SIDES)))
        if k == 0:
            own[2].wait()
            arrived(0, 2, range(len(SIDES)))
        advance(k, 0, None, 1, x_first - 2, x_first, True)
        advance(k, 0, None, 1, x_first, x_end, True, 0)
        advance(k, 0, None, 1, x_end, x_end + 2, True)
        advance(k, 1, 0, 0, x_first - 1, x_first, True)
        advance(k, 1, 0, 0, x_first, x_end, True, 1)
        advance(k, 1, 0, 0, x_end, x_end + 1, True)
        advance(k, 0, 1, 2, x_first, x_end, False, 2)
        send(1, k)

    def sum_message(turn, d):
        return pltpu.make_async_remote_copy(
            src_ref=partial.at[turn, places[turn]],
            dst_ref=partial.at[turn, places[turn]],
            send_sem=sum_send.at[turn, d],
            recv_sem=sum_recv.at[turn, d],
            device_id=partner(turn, d),
            device_id_type=MESH,
        )

    def sum_arrival(turn, d):
        place = (places[turn] + GROUP - d) % GROUP
        return pltpu.make_async_remote_copy(
            src_ref=partial.at[turn, place],
            dst_ref=partial.at[turn, place],
            send_sem=sum_send.at[turn, d],
            recv_sem=sum_recv.at[turn, d],
            device_id=partner(turn, d),
            device_id_type=MESH,
        )

    def sum_start(turn, row):
        partial[turn, places[turn]] = row
        for d in range(1, GROUP):
            sum_message(turn, d).start()

    def sum_finish(turn):
        for d in range(1, GROUP):
            sum_arrival(turn, d).wait_recv()
        row = partial[turn, 0]
        for place in range(1, GROUP):
            row = row + partial[turn, place]
        return row

    def own_moments():
        lanes = lax.broadcasted_iota(jnp.int32, (1, nz), 1)
        row = jnp.zeros((1, nz), jnp.float32)
        for k in range(2):
            for i in range(ITERS + 1):
                total = sums[k, i]
                if i >= 2:
                    total = 2.0 * total - sums[k, i % 2]
                total = jnp.sum(total, axis=0, keepdims=True)
                total = jnp.sum(total, axis=1, keepdims=True) / jnp.float32(sites)
                row = row + jnp.where(lanes == k * (nz // 2) + i, total, 0.0)
        return row

    for e in range(1, len(WIDTHS)):
        now, after = buffers[e], (1, 2, 1)[e - 1]
        moment = 3 if e == 1 else None
        later = 4 if e == 1 else None
        for k in range(2):
            arrived(e, k, Y_SIDES)
            advance(k, now, 0, 0, x_first + 1, x_end - 1, True, moment)
            if e >= 2:
                sent(e - 1, k)
            advance(k, 0, now, after, x_first + 2, x_end - 2, False, later)
        if e == 3:
            sum_start(2, sum_finish(1))
        for k in range(2):
            arrived(e, k, X_SIDES)
            advance(k, now, 0, 0, x_first - 1, x_first, True)
            advance(k, now, 0, 0, x_first, x_first + 1, True, moment)
            advance(k, 0, now, after, x_first, x_first + 2, False, later)
            advance(k, now, 0, 0, x_end - 1, x_end, True, moment)
            advance(k, now, 0, 0, x_end, x_end + 1, True)
            advance(k, 0, now, after, x_end - 2, x_end, False, later)
            if e + 1 < len(WIDTHS):
                send(e + 1, k)
            else:
                pltpu.make_async_copy(v.at[k, after, pl.ds(x_first, nx), pl.ds(ROW0, ny)], last_ref.at[k], local_sem.at[k]).start()
            if e == 2 and k == 0:
                sum_start(1, sum_finish(0))
        if e == 1:
            sum_start(0, own_moments())

    row = sum_finish(2)
    moments_ref[0:1, :] = row[:, : ITERS + 1]
    moments_ref[1:2, :] = pltpu.roll(row, nz // 2, 1)[:, : ITERS + 1]
    for k in range(3):
        sent(0, k)
    for k in range(2):
        sent(3, k)
    for turn in range(3):
        for d in range(1, GROUP):
            sum_message(turn, d).wait_send()
    for k in range(2):
        pltpu.make_async_copy(v.at[k, 1, pl.ds(x_first, nx), pl.ds(ROW0, ny)], last_ref.at[k], local_sem.at[k]).wait()


def local(random_vectors, disorder):
    vectors, nx, ny, nz = random_vectors.shape
    padded = (nx + 2 * HALO, ny + 2 * ROW0, nz)
    exchanges = (len(WIDTHS), vectors + 1, len(SIDES))
    return pl.pallas_call(
        body,
        out_shape=(
            jax.ShapeDtypeStruct((vectors, ITERS + 1), jnp.float32),
            jax.ShapeDtypeStruct(random_vectors.shape, jnp.float32),
        ),
        in_specs=[pl.BlockSpec(memory_space=pl.ANY)] * 2,
        out_specs=(pl.BlockSpec(memory_space=pltpu.VMEM), pl.BlockSpec(memory_space=pl.ANY)),
        scratch_shapes=[
            pltpu.VMEM((vectors, 3, *padded), jnp.float32),
            pltpu.VMEM(padded, jnp.float32),
            pltpu.VMEM((vectors, ITERS + 1, TILE, nz), jnp.float32),
            pltpu.VMEM((3, GROUP, 1, nz), jnp.float32),
            pltpu.SemaphoreType.DMA((3,)),
            pltpu.SemaphoreType.DMA(exchanges),
            pltpu.SemaphoreType.DMA(exchanges),
            pltpu.SemaphoreType.DMA((3, GROUP)),
            pltpu.SemaphoreType.DMA((3, GROUP)),
        ],
        compiler_params=pltpu.CompilerParams(collective_id=0, has_side_effects=True, vmem_limit_bytes=48 * 2**20),
    )(random_vectors, disorder)


def solution(mesh):
    placed = (P(None, "gx", "gy", None), P("gx", "gy", None))
    return jax.shard_map(
        local,
        mesh=mesh,
        in_specs=placed,
        out_specs=(P(), P(None, "gx", "gy", None)),
        check_vma=False,
    )
```

time: 314 us -> 76.7 us (0.24)
  the two profiles are of different devices: /device:TPU:6 before, /device:TPU:8 now
where the time goes in v1:
time: 76.7 us; the launch traced here: 76.5 us
  Pallas kernels  72.5 us (95%)
  local copies, waits for them, and re-layouts  3.34 us (4%)
    pallas_call x1, Pallas kernels, local(): pl.pallas_call(body, out_shape=(jax.ShapeDtypeStruct((vectors, ITERS + 1)...  72.5 us
    unnamed x6, local copies, waits for them, and re-layouts  3.34 us

profile of v1, /device:TPU:8, one launch (start us, length us, event | category | flops | bytes accessed | tf_op | source)
XLA Modules:
  0.0 76.5 jit_solution(13558361191458517754)
XLA Ops:
  0.6 0.0 copy-start
  0.6 1.0 %copy-done = f32[2,8,64,128]{3,2,1,0:T(8,128)S(1)} copy-done((f32[2,8,64,128]{3,2,1,0:T(8,128)S(1)}, f32[2,8,64,128]{3,2,1,0:T(8,128)}, u32[]{:S(2)}) %copy-start) | copy-done | bytes 524312
  1.7 0.0 copy-start.1
  1.7 0.9 %copy-done.1 = f32[8,64,128]{2,1,0:T(8,128)S(1)} copy-done((f32[8,64,128]{2,1,0:T(8,128)S(1)}, f32[8,64,128]{2,1,0:T(8,128)}, u32[]{:S(2)}) %copy-start.1) | copy-done | bytes 262168
  2.6 72.5 %shard_map.41 = (f32[2,10]{1,0:T(2,128)S(1)}, f32[2,8,64,128]{3,2,1,0:T(8,128)S(1)}) custom-call(f32[2,8,64,128]{3,2,1,0:T(8,128)S(1)} %copy-done, f32[8,64,128]{2,1,0:T(8,128)S(1)} %copy-done.1), custom_call_target="tpu_custom_call" | custom-call | tf_op jit(solution)/shard_map/pallas_call | solution.py:246
  75.1 0.6 copy.6
  75.7 0.8 %copy.7 = f32[2,8,64,128]{3,2,1,0:T(8,128)} copy(f32[2,8,64,128]{3,2,1,0:T(8,128)S(1)} %get-tuple-element.5) | data formatting | bytes 1048576
Async XLA Ops:
  0.6 1.0 %copy-start = (f32[2,8,64,128]{3,2,1,0:T(8,128)S(1)}, f32[2,8,64,128]{3,2,1,0:T(8,128)}, u32[]{:S(2)}) copy-start(f32[2,8,64,128]{3,2,1,0:T(8,128)} %start_ref.1) | copy-start | bytes 1572868
  1.7 0.9 %copy-start.1 = (f32[8,64,128]{2,1,0:T(8,128)S(1)}, f32[8,64,128]{2,1,0:T(8,128)}, u32[]{:S(2)}) copy-start(f32[8,64,128]{2,1,0:T(8,128)} %disorder_ref.1) | copy-start | bytes 786436

commit v2 on v1

v2 whole, which is shorter than its diff:
```python
import functools

import jax
import jax.numpy as jnp
from jax import lax
from jax.experimental import pallas as pl
from jax.experimental.pallas import tpu as pltpu
from jax.sharding import PartitionSpec as P

MESH = pl.DeviceIdType.MESH
ITERS = 9
ENERGY_SCALE = 10.5
TILE = 8
HALO = 3
ROW0 = 2 * TILE
PARITIES = 2
WIDTHS = (3, 2, 2, 2)
SIDES = ((-1, 0), (1, 0), (0, -1), (0, 1), (-1, -1), (-1, 1), (1, -1), (1, 1))
X_SIDES = (0, 1, 4, 5, 6, 7)
Y_SIDES = (2, 3)
GROUP = 8


def body(start_ref, disorder_ref, moments_ref, last_ref, v, energy, sums, partial, local_sem, send_sem, recv_sem, sum_send, sum_recv):
    _, nx, ny, nz = start_ref.shape
    sx, sy = lax.axis_size("gx"), lax.axis_size("gy")
    gx, gy = lax.axis_index("gx"), lax.axis_index("gy")
    x_first, x_end = HALO, HALO + nx
    y_end = ROW0 + ny
    sites = nx * ny * nz * sx * sy

    def beside(dx, dy):
        return (lax.rem(gx + sx + dx, sx), lax.rem(gy + sy + dy, sy))

    z, y_hi = gx // 4, gx % 4
    y_lo, xc = gy // GROUP, gy % GROUP
    y = y_hi * 2 + y_lo
    places = (xc, y, z)

    def partner(turn, d):
        if turn == 0:
            return (gx, y_lo * GROUP + (xc + d) % GROUP)
        if turn == 1:
            to = (y + d) % GROUP
            return (z * 4 + to // 2, (to % 2) * GROUP + xc)
        return (((z + d) % GROUP) * 4 + y_hi, gy)

    barrier = pltpu.get_barrier_semaphore()
    for dx, dy in reversed(SIDES):
        pl.semaphore_signal(barrier, inc=1, device_id=beside(dx, dy), device_id_type=MESH)
    for turn in reversed(range(3)):
        for d in range(1, GROUP):
            pl.semaphore_signal(barrier, inc=1, device_id=partner(turn, d), device_id_type=MESH)

    own = [pltpu.make_async_copy(start_ref.at[k], v.at[k, 0, pl.ds(x_first, nx), pl.ds(ROW0, ny)], local_sem.at[k]) for k in range(2)]
    own.append(pltpu.make_async_copy(disorder_ref, energy.at[pl.ds(x_first, nx), pl.ds(ROW0, ny)], local_sem.at[2]))
    for copy in own:
        copy.start()
    pl.semaphore_wait(barrier, len(SIDES) + 3 * (GROUP - 1))

    buffers = (0, 2, 1, 2)

    def message(e, k, side):
        dx, dy = SIDES[side]
        width = WIDTHS[e] - (k == 2) - (dx != 0 and dy != 0)
        x_from, x_size, x_to = {
            -1: (0, width, x_end),
            0: (0, nx, x_first),
            1: (nx - width, width, x_first - width),
        }[dx]
        y_from, y_size, y_to = {
            -1: (0, width, y_end),
            0: (0, ny, ROW0),
            1: (ny - width, width, ROW0 - width),
        }[dy]
        here = (pl.ds(x_from, x_size), pl.ds(y_from, y_size))
        there = (pl.ds(x_to, x_size), pl.ds(y_to, y_size))
        if k == 2:
            src, dst = disorder_ref.at[here], energy.at[there]
        else:
            b = buffers[e]
            if e == 0:
                src = start_ref.at[(k, *here)]
            else:
                src = v.at[k, b, pl.ds(x_first + x_from, x_size), pl.ds(ROW0 + y_from, y_size)]
            dst = v.at[(k, b, *there)]
        return pltpu.make_async_remote_copy(
            src_ref=src,
            dst_ref=dst,
            send_sem=send_sem.at[e % PARITIES, k],
            recv_sem=recv_sem.at[e % PARITIES, k, int(side in X_SIDES)],
            device_id=beside(dx, dy),
            device_id_type=MESH,
        )

    def send(e, k):
        for side in range(len(SIDES)):
            message(e, k, side).start()

    def rows_of(e, k, sides):
        total = 0
        for side in sides:
            dx, dy = SIDES[side]
            width = WIDTHS[e] - (k == 2) - (dx != 0 and dy != 0)
            total += (width if dx else nx) * (width if dy else ny)
        return total

    def wait_for(rows, semaphore):
        planes = next(n for n in range(1, v.shape[2]) if rows % n == 0 and rows // n <= v.shape[3])
        whole = v.at[0, 0, pl.ds(0, planes), pl.ds(0, rows // planes)]
        pltpu.make_async_copy(whole, whole, semaphore).wait()

    def arrived(e, k, sides):
        wait_for(rows_of(e, k, sides), recv_sem.at[e % PARITIES, k, int(sides == X_SIDES)])

    def sent(e, k):
        wait_for(rows_of(e, k, range(len(SIDES))), send_sem.at[e % PARITIES, k])

    def advance(k, now, before, after, x0, x1, wide, moment=None):
        r0, r1 = (ROW0 - TILE, y_end + TILE) if wide else (ROW0, y_end)
        factor = (1.0 if before is None else 2.0) / ENERGY_SCALE
        layers, rows = pl.ds(x0, x1 - x0), pl.ds(r0, r1 - r0)
        center = v[k, now, layers, rows, :]
        total = v[k, now, pl.ds(x0 + 1, x1 - x0), rows, :] + v[k, now, pl.ds(x0 - 1, x1 - x0), rows, :]
        total = total + v[k, now, layers, pl.ds(r0 + 1, r1 - r0), :] + v[k, now, layers, pl.ds(r0 - 1, r1 - r0), :]
        total = total + pltpu.roll(center, nz - 1, 2) + pltpu.roll(center, 1, 2)
        result = (energy[layers, rows, :] * center - total) * factor
        if before is not None:
            result = result - v[k, before, layers, rows, :]
        if after is None:
            last_ref[k, pl.ds(x0 - x_first, x1 - x0)] = result
        else:
            v[k, after, layers, rows, :] = result
        if moment is not None:
            if wide:
                center, result = center[:, TILE:-TILE], result[:, TILE:-TILE]
            for i, product in enumerate((center * center, center * result)):
                sums[k, 2 * moment + i] += jnp.sum(product.reshape(-1, TILE, nz), axis=0)

    sums[...] = jnp.zeros_like(sums)
    send(0, 2)
    send(0, 0)
    send(0, 1)

    for k in range(2):
        own[k].wait()
        if k == 0:
            own[2].wait()
            arrived(0, 2, Y_SIDES)
            arrived(0, 2, X_SIDES)
        arrived(0, k, Y_SIDES)
        arrived(0, k, X_SIDES)
        advance(k, 0, None, 1, x_first - 2, x_first, True)
        advance(k, 0, None, 1, x_first, x_end, True, 0)
        advance(k, 0, None, 1, x_end, x_end + 2, True)
        advance(k, 1, 0, 0, x_first - 1, x_first, True)
        advance(k, 1, 0, 0, x_first, x_end, True, 1)
        advance(k, 1, 0, 0, x_end, x_end + 1, True)
        advance(k, 0, 1, 2, x_first, x_end, False, 2)
        send(1, k)

    def sum_message(turn, d):
        return pltpu.make_async_remote_copy(
            src_ref=partial.at[turn, places[turn]],
            dst_ref=partial.at[turn, places[turn]],
            send_sem=sum_send.at[turn],
            recv_sem=sum_recv.at[turn],
            device_id=partner(turn, d),
            device_id_type=MESH,
        )

    def sum_start(turn, row):
        partial[turn, places[turn]] = row
        for d in range(1, GROUP):
            sum_message(turn, d).start()

    def sum_finish(turn):
        others = partial.at[turn, pl.ds(0, GROUP - 1)]
        pltpu.make_async_copy(others, others, sum_recv.at[turn]).wait()
        row = partial[turn, 0]
        for place in range(1, GROUP):
            row = row + partial[turn, place]
        return row

    def own_moments():
        lanes = lax.broadcasted_iota(jnp.int32, (1, nz), 1)
        row = jnp.zeros((1, nz), jnp.float32)
        for k in range(2):
            for i in range(ITERS + 1):
                total = sums[k, i]
                if i >= 2:
                    total = 2.0 * total - sums[k, i % 2]
                total = jnp.sum(total, axis=0, keepdims=True)
                total = jnp.sum(total, axis=1, keepdims=True) / jnp.float32(sites)
                row = row + jnp.where(lanes == k * (nz // 2) + i, total, 0.0)
        return row

    for e in range(1, len(WIDTHS)):
        now, after = buffers[e], (1, 2, None)[e - 1]
        moment = 3 if e == 1 else None
        later = 4 if e == 1 else None
        for k in range(2):
            arrived(e, k, Y_SIDES)
            advance(k, now, 0, 0, x_first + 1, x_end - 1, True, moment)
            sent(e - 1, k)
            advance(k, 0, now, after, x_first + 2, x_end - 2, False, later)
            if e == 3 and k == 0:
                sum_start(2, sum_finish(1))
            arrived(e, k, X_SIDES)
            advance(k, now, 0, 0, x_first - 1, x_first, True)
            advance(k, now, 0, 0, x_first, x_first + 1, True, moment)
            advance(k, 0, now, after, x_first, x_first + 2, False, later)
            advance(k, now, 0, 0, x_end - 1, x_end, True, moment)
            advance(k, now, 0, 0, x_end, x_end + 1, True)
            advance(k, 0, now, after, x_end - 2, x_end, False, later)
            if e + 1 < len(WIDTHS):
                send(e + 1, k)
            if e == 2 and k == 0:
                sum_start(1, sum_finish(0))
        if e == 1:
            sum_start(0, own_moments())

    row = sum_finish(2)
    moments_ref[0:1, :] = row[:, : ITERS + 1]
    moments_ref[1:2, :] = pltpu.roll(row, nz // 2, 1)[:, : ITERS + 1]
    sent(0, 2)
    for k in range(2):
        sent(len(WIDTHS) - 1, k)
    for turn in range(3):
        others = partial.at[turn, pl.ds(0, GROUP - 1)]
        pltpu.make_async_copy(others, others, sum_send.at[turn]).wait()


def local(random_vectors, disorder):
    vectors, nx, ny, nz = random_vectors.shape
    padded = (nx + 2 * HALO, ny + 2 * ROW0, nz)
    return pl.pallas_call(
        body,
        out_shape=(
            pltpu.VMEM((vectors, ITERS + 1), jnp.float32),
            pltpu.VMEM(random_vectors.shape, jnp.float32),
        ),
        in_specs=[pl.BlockSpec(memory_space=pltpu.HBM)] * 2,
        out_specs=(pl.BlockSpec(memory_space=pltpu.VMEM), pl.BlockSpec(memory_space=pltpu.VMEM)),
        scratch_shapes=[
            pltpu.VMEM((vectors, 3, *padded), jnp.float32),
            pltpu.VMEM(padded, jnp.float32),
            pltpu.VMEM((vectors, ITERS + 1, TILE, nz), jnp.float32),
            pltpu.VMEM((3, GROUP, 1, nz), jnp.float32),
            pltpu.SemaphoreType.DMA((3,)),
            pltpu.SemaphoreType.DMA((PARITIES, vectors + 1)),
            pltpu.SemaphoreType.DMA((PARITIES, vectors + 1, 2)),
            pltpu.SemaphoreType.DMA((3,)),
            pltpu.SemaphoreType.DMA((3,)),
        ],
        compiler_params=pltpu.CompilerParams(collective_id=0, has_side_effects=True, vmem_limit_bytes=60 * 2**20),
    )(random_vectors, disorder)


def solution(mesh):
    placed = (P(None, "gx", "gy", None), P("gx", "gy", None))
    return jax.shard_map(
        local,
        mesh=mesh,
        in_specs=placed,
        out_specs=(P(), P(None, "gx", "gy", None)),
        check_vma=False,
    )
```

time: 76.7 us -> 58.2 us (0.76)
  the two profiles are of different devices: /device:TPU:8 before, /device:TPU:1 now
where the time goes in v2:
time: 58.2 us; the launch traced here: 58 us
  Pallas kernels  56 us (96%)
  local copies, waits for them, and re-layouts  1.36 us (2%)
  between operations  0.64 us (1%)
    pallas_call x1, Pallas kernels, local(): pl.pallas_call(body, out_shape=(pltpu.VMEM((vectors, ITERS + 1), jnp.floa...  56 us
    unnamed x2, local copies, waits for them, and re-layouts  1.36 us

profile of v2, /device:TPU:1, one launch (start us, length us, event | category | flops | bytes accessed | tf_op | source)
XLA Modules:
  0.0 58.0 jit_solution(11412803204015218692)
XLA Ops:
  0.6 56.0 %shard_map.41 = (f32[2,10]{1,0:T(2,128)S(1)}, f32[2,8,64,128]{3,2,1,0:T(8,128)S(1)}) custom-call(f32[2,8,64,128]{3,2,1,0:T(8,128)} %start_ref.1, f32[8,64,128]{2,1,0:T(8,128)} %disorder_ref.1), custom_call_target="tpu_custom_call" | custom-call | tf_op jit(solution)/shard_map/pallas_call | solution.py:237
  56.7 0.6 copy.6
  57.2 0.8 %copy.7 = f32[2,8,64,128]{3,2,1,0:T(8,128)} copy(f32[2,8,64,128]{3,2,1,0:T(8,128)S(1)} %get-tuple-element.3) | data formatting | bytes 1048576

commit v3 on v2

--- a/solution.py
+++ b/solution.py
@@ -11,10 +11,10 @@
 ITERS = 9
 ENERGY_SCALE = 10.5
 TILE = 8
-HALO = 3
+HALO = 2
 ROW0 = 2 * TILE
 PARITIES = 2
-WIDTHS = (3, 2, 2, 2)
+WIDTHS = (1, 2, 2, 2, 2)
 SIDES = ((-1, 0), (1, 0), (0, -1), (0, 1), (-1, -1), (-1, 1), (1, -1), (1, 1))
 X_SIDES = (0, 1, 4, 5, 6, 7)
 Y_SIDES = (2, 3)
@@ -58,11 +58,11 @@
         copy.start()
     pl.semaphore_wait(barrier, len(SIDES) + 3 * (GROUP - 1))
 
-    buffers = (0, 2, 1, 2)
+    buffers = (0, 1, 2, 1, 2)
 
     def message(e, k, side):
         dx, dy = SIDES[side]
-        width = WIDTHS[e] - (k == 2) - (dx != 0 and dy != 0)
+        width = WIDTHS[e] - (dx != 0 and dy != 0)
         x_from, x_size, x_to = {
             -1: (0, width, x_end),
             0: (0, nx, x_first),
@@ -93,15 +93,18 @@
             device_id_type=MESH,
         )
 
+    def sides_of(e, within=range(len(SIDES))):
+        return [side for side in within if WIDTHS[e] > 1 or 0 in SIDES[side]]
+
     def send(e, k):
-        for side in range(len(SIDES)):
+        for side in reversed(sides_of(e)):
             message(e, k, side).start()
 
-    def rows_of(e, k, sides):
+    def rows_of(e, sides):
         total = 0
-        for side in sides:
+        for side in sides_of(e, sides):
             dx, dy = SIDES[side]
-            width = WIDTHS[e] - (k == 2) - (dx != 0 and dy != 0)
+            width = WIDTHS[e] - (dx != 0 and dy != 0)
             total += (width if dx else nx) * (width if dy else ny)
         return total
 
@@ -111,10 +114,10 @@
         pltpu.make_async_copy(whole, whole, semaphore).wait()
 
     def arrived(e, k, sides):
-        wait_for(rows_of(e, k, sides), recv_sem.at[e % PARITIES, k, int(sides == X_SIDES)])
+        wait_for(rows_of(e, sides), recv_sem.at[e % PARITIES, k, int(sides == X_SIDES)])
 
     def sent(e, k):
-        wait_for(rows_of(e, k, range(len(SIDES))), send_sem.at[e % PARITIES, k])
+        wait_for(rows_of(e, range(len(SIDES))), send_sem.at[e % PARITIES, k])
 
     def advance(k, now, before, after, x0, x1, wide, moment=None):
         r0, r1 = (ROW0 - TILE, y_end + TILE) if wide else (ROW0, y_end)
@@ -134,29 +137,24 @@
         if moment is not None:
             if wide:
                 center, result = center[:, TILE:-TILE], result[:, TILE:-TILE]
+            of_own = slice(max(x_first - x0, 0), min(x_end, x1) - x0)
+            center, result = center[of_own], result[of_own]
             for i, product in enumerate((center * center, center * result)):
                 sums[k, 2 * moment + i] += jnp.sum(product.reshape(-1, TILE, nz), axis=0)
 
     sums[...] = jnp.zeros_like(sums)
-    send(0, 2)
-    send(0, 0)
-    send(0, 1)
+    for k in range(3):
+        send(0, k)
 
     for k in range(2):
         own[k].wait()
         if k == 0:
             own[2].wait()
-            arrived(0, 2, Y_SIDES)
-            arrived(0, 2, X_SIDES)
         arrived(0, k, Y_SIDES)
+        advance(k, 0, None, 1, x_first + 1, x_end - 1, False, 0)
         arrived(0, k, X_SIDES)
-        advance(k, 0, None, 1, x_first - 2, x_first, True)
-        advance(k, 0, None, 1, x_first, x_end, True, 0)
-        advance(k, 0, None, 1, x_end, x_end + 2, True)
-        advance(k, 1, 0, 0, x_first - 1, x_first, True)
-        advance(k, 1, 0, 0, x_first, x_end, True, 1)
-        advance(k, 1, 0, 0, x_end, x_end + 1, True)
-        advance(k, 0, 1, 2, x_first, x_end, False, 2)
+        advance(k, 0, None, 1, x_first, x_first + 1, False, 0)
+        advance(k, 0, None, 1, x_end - 1, x_end, False, 0)
         send(1, k)
 
     def sum_message(turn, d):
@@ -196,28 +194,29 @@
         return row
 
     for e in range(1, len(WIDTHS)):
-        now, after = buffers[e], (1, 2, None)[e - 1]
-        moment = 3 if e == 1 else None
-        later = 4 if e == 1 else None
+        now, after = buffers[e], (2, 1, 2, None)[e - 1]
+        moment, later = ((1, 2), (3, 4), (None, None), (None, None))[e - 1]
         for k in range(2):
+            if e == 1 and k == 0:
+                arrived(0, 2, Y_SIDES)
             arrived(e, k, Y_SIDES)
             advance(k, now, 0, 0, x_first + 1, x_end - 1, True, moment)
             sent(e - 1, k)
             advance(k, 0, now, after, x_first + 2, x_end - 2, False, later)
-            if e == 3 and k == 0:
+            if e == 4 and k == 0:
                 sum_start(2, sum_finish(1))
+            if e == 1 and k == 0:
+                arrived(0, 2, X_SIDES)
             arrived(e, k, X_SIDES)
-            advance(k, now, 0, 0, x_first - 1, x_first, True)
-            advance(k, now, 0, 0, x_first, x_first + 1, True, moment)
+            advance(k, now, 0, 0, x_first - 1, x_first + 1, True, moment)
+            advance(k, now, 0, 0, x_end - 1, x_end + 1, True, moment)
             advance(k, 0, now, after, x_first, x_first + 2, False, later)
-            advance(k, now, 0, 0, x_end - 1, x_end, True, moment)
-            advance(k, now, 0, 0, x_end, x_end + 1, True)
             advance(k, 0, now, after, x_end - 2, x_end, False, later)
             if e + 1 < len(WIDTHS):
                 send(e + 1, k)
-            if e == 2 and k == 0:
+            if e == 3 and k == 0:
                 sum_start(1, sum_finish(0))
-        if e == 1:
+        if e == 2:
             sum_start(0, own_moments())
 
     row = sum_finish(2)
@@ -231,10 +230,19 @@
         pltpu.make_async_copy(others, others, sum_send.at[turn]).wait()
 
 
+def to_hbm(moments_ref, last_ref, moments_out, last_out, sems):
+    copies = [pltpu.make_async_copy(moments_ref, moments_out, sems.at[0])]
+    copies += [pltpu.make_async_copy(last_ref.at[k], last_out.at[k], sems.at[k + 1]) for k in range(2)]
+    for copy in copies:
+        copy.start()
+    for copy in copies:
+        copy.wait()
+
+
 def local(random_vectors, disorder):
     vectors, nx, ny, nz = random_vectors.shape
     padded = (nx + 2 * HALO, ny + 2 * ROW0, nz)
-    return pl.pallas_call(
+    outputs = pl.pallas_call(
         body,
         out_shape=(
             pltpu.VMEM((vectors, ITERS + 1), jnp.float32),
@@ -255,6 +263,17 @@
         ],
         compiler_params=pltpu.CompilerParams(collective_id=0, has_side_effects=True, vmem_limit_bytes=60 * 2**20),
     )(random_vectors, disorder)
+    return pl.pallas_call(
+        to_hbm,
+        out_shape=(
+            jax.ShapeDtypeStruct((vectors, ITERS + 1), jnp.float32),
+            jax.ShapeDtypeStruct(random_vectors.shape, jnp.float32),
+        ),
+        in_specs=[pl.BlockSpec(memory_space=pltpu.VMEM)] * 2,
+        out_specs=(pl.BlockSpec(memory_space=pltpu.HBM), pl.BlockSpec(memory_space=pltpu.HBM)),
+        scratch_shapes=[pltpu.SemaphoreType.DMA((vectors + 1,))],
+        compiler_params=pltpu.CompilerParams(vmem_limit_bytes=2**20),
+    )(*outputs)
 
 
 def solution(mesh):

time: 58.2 us -> 54.4 us (0.935)
  the two profiles are of different devices: /device:TPU:1 before, /device:TPU:6 now
where the time goes in v3:
time: 54.4 us; the launch traced here: 54 us
  Pallas kernels  53.4 us (98%)
  between operations  0.64 us (1%)
    pallas_call x1, Pallas kernels, local(): pl.pallas_call(body, out_shape=(pltpu.VMEM((vectors, ITERS + 1), jnp.floa...  52.6 us

profile of v3, /device:TPU:6, one launch (start us, length us, event | category | flops | bytes accessed | tf_op | source)
XLA Modules:
  0.0 54.0 jit_solution(10178044276125512674)
XLA Ops:
  0.6 52.6 %shard_map.41 = (f32[2,10]{1,0:T(2,128)S(1)}, f32[2,8,64,128]{3,2,1,0:T(8,128)S(1)}) custom-call(f32[2,8,64,128]{3,2,1,0:T(8,128)} %start_ref.1, f32[8,64,128]{2,1,0:T(8,128)} %disorder_ref.1), custom_call_target="tpu_custom_call" | custom-call | tf_op jit(solution)/shard_map/pallas_call | solution.py:245
  53.2 0.8 %shard_map.42 = (f32[2,10]{1,0:T(2,128)}, f32[2,8,64,128]{3,2,1,0:T(8,128)}) custom-call(f32[2,10]{1,0:T(2,128)S(1)} %get-tuple-element.4.moments_ref, f32[2,8,64,128]{3,2,1,0:T(8,128)S(1)} %get-tuple-element.5.last_ref), custom_call_target="tpu_custom_call" | custom-call | tf_op jit(solution)/shard_map/pallas_call | solution.py:266

commit v4 on v3

--- a/solution.py
+++ b/solution.py
@@ -15,9 +15,11 @@
 ROW0 = 2 * TILE
 PARITIES = 2
 WIDTHS = (1, 2, 2, 2, 2)
+ENDS = (0, 18, 17, 16, 15)
 SIDES = ((-1, 0), (1, 0), (0, -1), (0, 1), (-1, -1), (-1, 1), (1, -1), (1, 1))
 X_SIDES = (0, 1, 4, 5, 6, 7)
 Y_SIDES = (2, 3)
+X_FACES = (0, 1)
 GROUP = 8
 
 
@@ -60,7 +62,7 @@
 
     buffers = (0, 1, 2, 1, 2)
 
-    def message(e, k, side):
+    def message(e, k, side, part=None):
         dx, dy = SIDES[side]
         width = WIDTHS[e] - (dx != 0 and dy != 0)
         x_from, x_size, x_to = {
@@ -73,6 +75,9 @@
             0: (0, ny, ROW0),
             1: (ny - width, width, ROW0 - width),
         }[dy]
+        if part is not None:
+            y_from, y_size = ((0, ENDS[e]), (ny - ENDS[e], ENDS[e]), (ENDS[e], ny - 2 * ENDS[e]))[part]
+            y_to = ROW0 + y_from
         here = (pl.ds(x_from, x_size), pl.ds(y_from, y_size))
         there = (pl.ds(x_to, x_size), pl.ds(y_to, y_size))
         if k == 2:
@@ -88,7 +93,7 @@
             src_ref=src,
             dst_ref=dst,
             send_sem=send_sem.at[e % PARITIES, k],
-            recv_sem=recv_sem.at[e % PARITIES, k, int(side in X_SIDES)],
+            recv_sem=recv_sem.at[e % PARITIES, k, 2 if part == 2 else int(side in X_SIDES)],
             device_id=beside(dx, dy),
             device_id_type=MESH,
         )
@@ -98,7 +103,15 @@
 
     def send(e, k):
         for side in reversed(sides_of(e)):
-            message(e, k, side).start()
+            if e > 0 and side in X_FACES:
+                for part in range(2):
+                    message(e, k, side, part).start()
+            else:
+                message(e, k, side).start()
+
+    def send_middle(e, k):
+        for side in X_FACES:
+            message(e, k, side, 2).start()
 
     def rows_of(e, sides):
         total = 0
@@ -113,14 +126,21 @@
         whole = v.at[0, 0, pl.ds(0, planes), pl.ds(0, rows // planes)]
         pltpu.make_async_copy(whole, whole, semaphore).wait()
 
+    def middle_rows(e):
+        return 2 * WIDTHS[e] * (ny - 2 * ENDS[e]) if e > 0 else 0
+
     def arrived(e, k, sides):
-        wait_for(rows_of(e, sides), recv_sem.at[e % PARITIES, k, int(sides == X_SIDES)])
+        rows = rows_of(e, sides) - (middle_rows(e) if sides == X_SIDES else 0)
+        wait_for(rows, recv_sem.at[e % PARITIES, k, int(sides == X_SIDES)])
+
+    def middle_arrived(e, k):
+        wait_for(middle_rows(e), recv_sem.at[e % PARITIES, k, 2])
 
     def sent(e, k):
         wait_for(rows_of(e, range(len(SIDES))), send_sem.at[e % PARITIES, k])
 
-    def advance(k, now, before, after, x0, x1, wide, moment=None):
-        r0, r1 = (ROW0 - TILE, y_end + TILE) if wide else (ROW0, y_end)
+    def advance(k, now, before, after, x0, x1, wide, moment=None, between=None):
+        r0, r1 = between or ((ROW0 - TILE, y_end + TILE) if wide else (ROW0, y_end))
         factor = (1.0 if before is None else 2.0) / ENERGY_SCALE
         layers, rows = pl.ds(x0, x1 - x0), pl.ds(r0, r1 - r0)
         center = v[k, now, layers, rows, :]
@@ -139,11 +159,27 @@
                 center, result = center[:, TILE:-TILE], result[:, TILE:-TILE]
             of_own = slice(max(x_first - x0, 0), min(x_end, x1) - x0)
             center, result = center[of_own], result[of_own]
-            for i, product in enumerate((center * center, center * result)):
-                sums[k, 2 * moment + i] += jnp.sum(product.reshape(-1, TILE, nz), axis=0)
+            add_moments(k, moment, center, result)
+
+    def add_moments(k, moment, center, result):
+        for i, product in enumerate((center * center, center * result)):
+            sums[k, 2 * moment + i] += jnp.sum(product.reshape(-1, TILE, nz), axis=0)
+
+    def record(k, now, after, x0, x1, moment):
+        at = (pl.ds(x0, x1 - x0), pl.ds(ROW0, ny))
+        add_moments(k, moment, v[(k, now, *at)], v[(k, after, *at)])
+
+    def edges(k, now, after, spans_outer, spans_first, spans_next):
+        for spans, layers in ((spans_outer, (x_first - 1, x_end)), (spans_first, (x_first, x_end - 1))):
+            for x in layers:
+                for span in spans:
+                    advance(k, now, 0, 0, x, x + 1, False, between=span)
+        for x in (x_first, x_end - 2):
+            for span in spans_next:
+                advance(k, 0, now, after, x, x + 2, False, between=span)
 
     sums[...] = jnp.zeros_like(sums)
-    for k in range(3):
+    for k in (0, 2, 1):
         send(0, k)
 
     for k in range(2):
@@ -156,6 +192,7 @@
         advance(k, 0, None, 1, x_first, x_first + 1, False, 0)
         advance(k, 0, None, 1, x_end - 1, x_end, False, 0)
         send(1, k)
+        send_middle(1, k)
 
     def sum_message(turn, d):
         return pltpu.make_async_remote_copy(
@@ -208,12 +245,25 @@
             if e == 1 and k == 0:
                 arrived(0, 2, X_SIDES)
             arrived(e, k, X_SIDES)
-            advance(k, now, 0, 0, x_first - 1, x_first + 1, True, moment)
-            advance(k, now, 0, 0, x_end - 1, x_end + 1, True, moment)
-            advance(k, 0, now, after, x_first, x_first + 2, False, later)
-            advance(k, 0, now, after, x_end - 2, x_end, False, later)
             if e + 1 < len(WIDTHS):
+                low, high = ROW0 + ENDS[e + 1], y_end - ENDS[e + 1]
+                ends = ((ROW0, low), (high, y_end))
+                edges(k, now, after, ends, ((ROW0 - TILE, low + 1), (high - 1, y_end + TILE)), ends)
                 send(e + 1, k)
+                middle_arrived(e, k)
+                edges(k, now, after, ((low, high),), ((low + 1, high - 1),), ((low, high),))
+                send_middle(e + 1, k)
+                if moment is not None:
+                    for x in (x_first, x_end - 1):
+                        record(k, now, 0, x, x + 1, moment)
+                    for x in (x_first, x_end - 2):
+                        record(k, 0, after, x, x + 2, later)
+            else:
+                middle_arrived(e, k)
+                advance(k, now, 0, 0, x_first - 1, x_first + 1, True)
+                advance(k, now, 0, 0, x_end - 1, x_end + 1, True)
+                advance(k, 0, now, after, x_first, x_first + 2, False)
+                advance(k, 0, now, after, x_end - 2, x_end, False)
             if e == 3 and k == 0:
                 sum_start(1, sum_finish(0))
         if e == 2:
@@ -257,7 +307,7 @@
             pltpu.VMEM((3, GROUP, 1, nz), jnp.float32),
             pltpu.SemaphoreType.DMA((3,)),
             pltpu.SemaphoreType.DMA((PARITIES, vectors + 1)),
-            pltpu.SemaphoreType.DMA((PARITIES, vectors + 1, 2)),
+            pltpu.SemaphoreType.DMA((PARITIES, vectors + 1, 3)),
             pltpu.SemaphoreType.DMA((3,)),
             pltpu.SemaphoreType.DMA((3,)),
         ],

time: 54.4 us -> 53.3 us (0.980)
  Pallas kernels: 53.4 us -> 52.5 us
    pallas_call x1, Pallas kernels: 52.6 us -> 51.7 us  [local(): pl.pallas_call(body, out_shape=(pltpu.VMEM((vectors, ITERS + 1), jnp.floa...]
where the time goes in v4:
time: 53.3 us; the launch traced here: 53.1 us
  Pallas kernels  52.5 us (98%)
  between operations  0.64 us (1%)
    pallas_call x1, Pallas kernels, local(): pl.pallas_call(body, out_shape=(pltpu.VMEM((vectors, ITERS + 1), jnp.floa...  51.7 us

profile of v4, /device:TPU:6, one launch (start us, length us, event | category | flops | bytes accessed | tf_op | source)
XLA Modules:
  0.0 53.1 jit_solution(485089972278151474)
XLA Ops:
  0.6 51.7 %shard_map.41 = (f32[2,10]{1,0:T(2,128)S(1)}, f32[2,8,64,128]{3,2,1,0:T(8,128)S(1)}) custom-call(f32[2,8,64,128]{3,2,1,0:T(8,128)} %start_ref.1, f32[8,64,128]{2,1,0:T(8,128)} %disorder_ref.1), custom_call_target="tpu_custom_call" | custom-call | tf_op jit(solution)/shard_map/pallas_call | solution.py:295
  52.3 0.8 %shard_map.42 = (f32[2,10]{1,0:T(2,128)}, f32[2,8,64,128]{3,2,1,0:T(8,128)}) custom-call(f32[2,10]{1,0:T(2,128)S(1)} %get-tuple-element.4.moments_ref, f32[2,8,64,128]{3,2,1,0:T(8,128)S(1)} %get-tuple-element.5.last_ref), custom_call_target="tpu_custom_call" | custom-call | tf_op jit(solution)/shard_map/pallas_call | solution.py:316

commit v5 on v4

--- a/solution.py
+++ b/solution.py
@@ -250,6 +250,8 @@
                 ends = ((ROW0, low), (high, y_end))
                 edges(k, now, after, ends, ((ROW0 - TILE, low + 1), (high - 1, y_end + TILE)), ends)
                 send(e + 1, k)
+                if e == 3 and k == 0:
+                    sum_start(1, sum_finish(0))
                 middle_arrived(e, k)
                 edges(k, now, after, ((low, high),), ((low + 1, high - 1),), ((low, high),))
                 send_middle(e + 1, k)
@@ -264,8 +266,6 @@
                 advance(k, now, 0, 0, x_end - 1, x_end + 1, True)
                 advance(k, 0, now, after, x_first, x_first + 2, False)
                 advance(k, 0, now, after, x_end - 2, x_end, False)
-            if e == 3 and k == 0:
-                sum_start(1, sum_finish(0))
         if e == 2:
             sum_start(0, own_moments())
 

time: 53.3 us -> 52.7 us (0.989)
  Pallas kernels: 52.5 us -> 51.8 us
    pallas_call x1, Pallas kernels: 51.7 us -> 50.9 us  [local(): pl.pallas_call(body, out_shape=(pltpu.VMEM((vectors, ITERS + 1), jnp.floa...]
where the time goes in v5:
time: 52.7 us; the launch traced here: 52.4 us
  Pallas kernels  51.8 us (98%)
  between operations  0.64 us (1%)
    pallas_call x1, Pallas kernels, local(): pl.pallas_call(body, out_shape=(pltpu.VMEM((vectors, ITERS + 1), jnp.floa...  50.9 us

profile of v5, /device:TPU:6, one launch (start us, length us, event | category | flops | bytes accessed | tf_op | source)
XLA Modules:
  0.0 52.4 jit_solution(2817316692211571447)
XLA Ops:
  0.6 50.9 %shard_map.41 = (f32[2,10]{1,0:T(2,128)S(1)}, f32[2,8,64,128]{3,2,1,0:T(8,128)S(1)}) custom-call(f32[2,8,64,128]{3,2,1,0:T(8,128)} %start_ref.1, f32[8,64,128]{2,1,0:T(8,128)} %disorder_ref.1), custom_call_target="tpu_custom_call" | custom-call | tf_op jit(solution)/shard_map/pallas_call | solution.py:295
  51.6 0.8 %shard_map.42 = (f32[2,10]{1,0:T(2,128)}, f32[2,8,64,128]{3,2,1,0:T(8,128)}) custom-call(f32[2,10]{1,0:T(2,128)S(1)} %get-tuple-element.4.moments_ref, f32[2,8,64,128]{3,2,1,0:T(8,128)S(1)} %get-tuple-element.5.last_ref), custom_call_target="tpu_custom_call" | custom-call | tf_op jit(solution)/shard_map/pallas_call | solution.py:316

commit v6 on v4

--- a/solution.py
+++ b/solution.py
@@ -15,7 +15,7 @@
 ROW0 = 2 * TILE
 PARITIES = 2
 WIDTHS = (1, 2, 2, 2, 2)
-ENDS = (0, 18, 17, 16, 15)
+ENDS = (0, 18, 17, 16, 15, 14)
 SIDES = ((-1, 0), (1, 0), (0, -1), (0, 1), (-1, -1), (-1, 1), (1, -1), (1, 1))
 X_SIDES = (0, 1, 4, 5, 6, 7)
 Y_SIDES = (2, 3)
@@ -151,7 +151,7 @@
         if before is not None:
             result = result - v[k, before, layers, rows, :]
         if after is None:
-            last_ref[k, pl.ds(x0 - x_first, x1 - x0)] = result
+            last_ref[k, pl.ds(x0 - x_first, x1 - x0), pl.ds(r0 - ROW0, r1 - r0)] = result
         else:
             v[k, after, layers, rows, :] = result
         if moment is not None:
@@ -245,27 +245,22 @@
             if e == 1 and k == 0:
                 arrived(0, 2, X_SIDES)
             arrived(e, k, X_SIDES)
+            low, high = ROW0 + ENDS[e + 1], y_end - ENDS[e + 1]
+            ends = ((ROW0, low), (high, y_end))
+            edges(k, now, after, ends, ((ROW0 - TILE, low + 1), (high - 1, y_end + TILE)), ends)
             if e + 1 < len(WIDTHS):
-                low, high = ROW0 + ENDS[e + 1], y_end - ENDS[e + 1]
-                ends = ((ROW0, low), (high, y_end))
-                edges(k, now, after, ends, ((ROW0 - TILE, low + 1), (high - 1, y_end + TILE)), ends)
                 send(e + 1, k)
-                middle_arrived(e, k)
-                edges(k, now, after, ((low, high),), ((low + 1, high - 1),), ((low, high),))
-                send_middle(e + 1, k)
-                if moment is not None:
-                    for x in (x_first, x_end - 1):
-                        record(k, now, 0, x, x + 1, moment)
-                    for x in (x_first, x_end - 2):
-                        record(k, 0, after, x, x + 2, later)
-            else:
-                middle_arrived(e, k)
-                advance(k, now, 0, 0, x_first - 1, x_first + 1, True)
-                advance(k, now, 0, 0, x_end - 1, x_end + 1, True)
-                advance(k, 0, now, after, x_first, x_first + 2, False)
-                advance(k, 0, now, after, x_end - 2, x_end, False)
             if e == 3 and k == 0:
                 sum_start(1, sum_finish(0))
+            middle_arrived(e, k)
+            edges(k, now, after, ((low, high),), ((low + 1, high - 1),), ((low, high),))
+            if e + 1 < len(WIDTHS):
+                send_middle(e + 1, k)
+            if moment is not None:
+                for x in (x_first, x_end - 1):
+                    record(k, now, 0, x, x + 1, moment)
+                for x in (x_first, x_end - 2):
+                    record(k, 0, after, x, x + 2, later)
         if e == 2:
             sum_start(0, own_moments())
 

time: 53.3 us -> 52.6 us (0.987)
  Pallas kernels: 52.5 us -> 51.8 us
    pallas_call x1, Pallas kernels: 51.7 us -> 50.9 us  [local(): pl.pallas_call(body, out_shape=(pltpu.VMEM((vectors, ITERS + 1), jnp.floa...]
where the time goes in v6:
time: 52.6 us; the launch traced here: 52.4 us
  Pallas kernels  51.8 us (98%)
  between operations  0.64 us (1%)
    pallas_call x1, Pallas kernels, local(): pl.pallas_call(body, out_shape=(pltpu.VMEM((vectors, ITERS + 1), jnp.floa...  50.9 us

profile of v6, /device:TPU:6, one launch (start us, length us, event | category | flops | bytes accessed | tf_op | source)
XLA Modules:
  0.0 52.4 jit_solution(7970680475006246313)
XLA Ops:
  0.6 50.9 %shard_map.41 = (f32[2,10]{1,0:T(2,128)S(1)}, f32[2,8,64,128]{3,2,1,0:T(8,128)S(1)}) custom-call(f32[2,8,64,128]{3,2,1,0:T(8,128)} %start_ref.1, f32[8,64,128]{2,1,0:T(8,128)} %disorder_ref.1), custom_call_target="tpu_custom_call" | custom-call | tf_op jit(solution)/shard_map/pallas_call | solution.py:290
  51.6 0.8 %shard_map.42 = (f32[2,10]{1,0:T(2,128)}, f32[2,8,64,128]{3,2,1,0:T(8,128)}) custom-call(f32[2,10]{1,0:T(2,128)S(1)} %get-tuple-element.4.moments_ref, f32[2,8,64,128]{3,2,1,0:T(8,128)S(1)} %get-tuple-element.5.last_ref), custom_call_target="tpu_custom_call" | custom-call | tf_op jit(solution)/shard_map/pallas_call | solution.py:311
